TPU v7x, 32 devices: a whole 2x2x4 slice. The times are simulated.
32 devices in a mesh: freq: 8 (over y, x, core), chan: 4 (over z).
Axes of the slice: x: 2, y: 2, z: 4, core: 2. Of those that a mesh axis runs over, the one named last changes fastest.
Arguments:
- factor: bfloat16 [512, 2, 128, 128], P('freq', None, 'chan'), may hold values from -0.2 to 1.2, as said below
- spectrum: bfloat16 [512, 2, 128, 128], P('freq', None, 'chan'), may hold values from -2 to 5, as said below
- guess_scale: float32 [512], P('freq'), may hold values from 0.1 to 0.3
- lag_cutoff: int32 [1], replicated, may hold values from 64 to 255
Outputs:
- new_factor: float32 [512, 2, 128, 128], P('freq', None, None, 'chan')
Inputs may be any that keep to these rules, and one draw needn't show every extreme that they name: The real part of factor is the identity plus independent entries of spread about 0.35 / sqrt(128). At every frequency spectrum is Hermitian: its real part symmetric, its imaginary part antisymmetric with a zero diagonal; it is positive definite.
All inputs are finite; a program needn't handle non-finite values.
Results may differ from a plain program's by a relative error of at most 0.00105.
Values may be sent and summed in bfloat16 or wider, within the bound.
No kernel may reach another device: no remote copies, remote signals or barrier semaphores. Data moves between devices by JAX's collectives and lax.ppermute only.
A program may use at most 128 MiB of HBM per device.

v0:
```python
import functools
import math

import jax
import jax.numpy as jnp
from jax import lax
from jax.experimental import pallas as pl
from jax.experimental.pallas import tpu as pltpu
from jax.sharding import PartitionSpec as P

ITERS = 8
SCALE = 16.0
CHUNKS = 1
F32 = jnp.float32
BF16 = jnp.bfloat16
MIB = 1024 * 1024
NN = (((1,), (0,)), ((), ()))
NT = (((1,), (1,)), ((), ()))
TN = (((0,), (0,)), ((), ()))


def dot(left, right, dims=NN):
    return lax.dot_general(left, right, dims, preferred_element_type=F32)


def split(value):
    high = value.astype(BF16)
    return high, (value - high.astype(F32)).astype(BF16)


def cat(parts, axis):
    return jnp.concatenate(parts, axis=axis)


def dot3(left_high, left_low, right_high, right_low, dims=NN):
    rows = left_high.shape[0]
    both = dot(cat([left_high, left_low], 0), right_high, dims)
    return both[:rows] + (both[rows:] + dot(left_high, right_low, dims))


def eye(size):
    rows = lax.broadcasted_iota(jnp.int32, (size, size), 0)
    columns = lax.broadcasted_iota(jnp.int32, (size, size), 1)
    return jnp.where(rows == columns, 1.0, 0.0).astype(F32)


def newton_kernel(scale_ref, psi_ref, out_ref):
    bins = psi_ref.shape[1]
    size = psi_ref.shape[4]
    identity = eye(size)
    state = []
    for item in range(bins):
        re = psi_ref[:, item, 0].reshape(size, size)
        im = psi_ref[:, item, 1].reshape(size, size)
        scale = scale_ref[pl.program_id(0) * bins + item]
        gram = dot(cat([re, im], 0), cat([cat([re, im], 1), cat([im, -re], 1)], 0), TN)
        sym = identity - scale * gram[:, :size]
        anti = -scale * gram[:, size:]
        state.append((sym, anti, None))
    for step in range(ITERS):
        after = []
        for sym, anti, total in state:
            left_high, left_low = split(cat([sym, anti], 1))
            if step == 0:
                total = identity + (sym + anti)
                right = cat([sym + anti, sym - anti], 0)
            elif step < ITERS - 1:
                right = cat([cat([sym + anti, total], 1), cat([sym - anti, total.T], 1)], 0)
            else:
                right = cat([total, total.T], 0)
            product = dot3(left_high, left_low, *split(right))
            if step > 0:
                total = total + product[:, -size:]
            if step < ITERS - 1:
                square = product[:, :size]
                square_t = square.T
                sym = 0.5 * (square + square_t)
                anti = 0.5 * (square - square_t)
            after.append((sym, anti, total))
        state = after
    for item in range(bins):
        total = state[item][2]
        total_t = total.T
        re = psi_ref[:, item, 0].reshape(size, size)
        im = psi_ref[:, item, 1].reshape(size, size)
        scale = scale_ref[pl.program_id(0) * bins + item]
        half = (0.5 * scale) * cat([total + total_t, total - total_t], 1)
        high, low = split(half)
        both = dot(cat([high, low], 0), cat([cat([re, im], 1), cat([-im, re], 1)], 0), NT)
        high, low = split(both[:size] + both[size:])
        out_ref[item, 0] = high
        out_ref[item, 1] = low


def middle_kernel(inverse_ref, packed_ref, out_ref):
    bins, size = inverse_ref.shape[0], inverse_ref.shape[2]
    total_bins = pl.num_programs(0) * bins
    identity = eye(size)
    rows = lax.broadcasted_iota(jnp.int32, (size, size), 0)
    columns = lax.broadcasted_iota(jnp.int32, (size, size), 1)
    for item in range(bins):
        packed = packed_ref[:, item].reshape(size, size).astype(F32)
        packed_t = packed.T
        re = jnp.where(columns >= rows, packed, packed_t).astype(BF16)
        im = jnp.where(columns == rows, 0.0, jnp.where(columns < rows, packed, -packed_t)).astype(BF16)
        high, low = inverse_ref[item, 0], inverse_ref[item, 1]
        both = dot(cat([high, low], 0), cat([cat([re, im], 1), cat([-im, re], 1)], 0))
        left = both[:size] + both[size:]
        left_re, left_im = left[:, :size], left[:, size:]
        left_high, left_low = split(cat([left_re + left_im, left_im - left_re], 1))
        middle = dot3(left_high, left_low, high, low, NT)
        place = pl.program_id(0) * bins + item
        out_ref[pl.ds(place, size, stride=total_bins), :] = (middle + identity) * (1.0 / SCALE)


def causal_kernel(table_ref, values_ref, out_ref, table_high, table_low):
    count = table_ref.shape[1]
    sources, kept, own, lanes = values_ref.shape

    @pl.when(pl.program_id(0) == 0)
    def _():
        for part in range(2):
            high, low = split(table_ref[part])
            table_high[part * count : (part + 1) * count] = high
            table_low[part * count : (part + 1) * count] = low

    values = cat([values_ref[:, item].reshape(count, lanes) for item in range(kept)], 1)
    high, low = split(values)
    whole = dot(table_high[...], high) + (dot(table_high[...], low) + dot(table_low[...], high))
    for item in range(kept):
        for part in range(2):
            piece = whole[part * count : (part + 1) * count, item * lanes : (item + 1) * lanes]
            out_ref[:, item, part] = piece.reshape(sources, own, lanes)


def product_kernel(causal_ref, psi_ref, out_ref):
    bins, size = psi_ref.shape[1], psi_ref.shape[4]
    total_bins = causal_ref.shape[0] // (2 * size)
    for item in range(bins):
        re = psi_ref[:, item, 0].reshape(size, size)
        im = psi_ref[:, item, 1].reshape(size, size)
        place = pl.program_id(0) * bins + item
        part_re = causal_ref[pl.ds(place, size, stride=2 * total_bins), :]
        part_im = causal_ref[pl.ds(total_bins + place, size, stride=2 * total_bins), :]
        added, taken = part_re + part_im, part_re - part_im
        high, low = split(0.5 * cat([taken.T + added, added.T - taken], 1))
        both = dot(cat([high, low], 0), cat([cat([re, -im], 1), cat([im, re], 1)], 0), NT)
        result = both[:size] + both[size:]
        shape = (psi_ref.shape[0], psi_ref.shape[3], size)
        out_ref[:, item, 0] = result[:, :size].reshape(shape)
        out_ref[:, item, 1] = result[:, size:].reshape(shape)


def owned_bins(index, own, freq_size, chan_size, chunks):
    part = own // chunks
    inner = index % own
    group = index // own % freq_size
    member = index // (own * freq_size)
    return group * (own * chan_size) + inner // part * (part * chan_size) + member * part + inner % part


def projection_table(lag_limit, count, freq_size, chan_size, chunks):
    own = count // (freq_size * chan_size)
    rows = lax.broadcasted_iota(jnp.int32, (count, 1), 0)
    columns = lax.broadcasted_iota(jnp.int32, (1, count), 1)
    shift = owned_bins(columns, own, freq_size, chan_size, chunks) - owned_bins(
        rows, own, freq_size, chan_size, chunks
    )
    unit = math.pi / count
    half_angle = shift.astype(F32) * unit
    turned = ((2 * lag_limit + 1) * shift) % (2 * count)
    turned = jnp.where(turned >= count, turned - 2 * count, turned)
    last_angle = turned.astype(F32) * unit
    below = jnp.where(shift == 0, 1.0, 2.0 * count * jnp.sin(half_angle))
    real = jnp.where(shift == 0, (lag_limit.astype(F32) + 0.5) / count, jnp.sin(last_angle) / below)
    imag = jnp.where(shift == 0, 0.0, (jnp.cos(half_angle) - jnp.cos(last_angle)) / below)
    return jnp.stack([real, imag])


def params(limit):
    return pltpu.CompilerParams(vmem_limit_bytes=limit * MIB)


def cost(flops, moved):
    return pl.CostEstimate(flops=flops, bytes_accessed=moved, transcendentals=0)


def shards(freq_size, chan_size, factor, spectrum, guess_scale, lag_cutoff):
    group_bins, _, rows, size = factor.shape
    own = group_bins // chan_size
    count = group_bins * freq_size
    chunks = CHUNKS if own % (8 * CHUNKS) == 0 else 1
    part = own // chunks
    step = math.gcd(part, 4)
    column_parts = min(freq_size, rows)
    lane_parts = freq_size // column_parts
    kept = rows // column_parts
    lanes = size // lane_parts
    member = lax.axis_index("chan")
    devices = chan_size * freq_size

    panel_block = pl.BlockSpec((chan_size, step, 2, rows, size), lambda i: (0, i, 0, 0, 0))
    inverse_block = pl.BlockSpec((step, 2, size, 2 * size), lambda i: (i, 0, 0, 0))

    owned = []
    for chunk in range(chunks):
        piece = factor[chunk * part * chan_size : (chunk + 1) * part * chan_size]
        if owned:
            piece, owned[-1] = lax.optimization_barrier((piece, owned[-1]))
        piece = lax.all_to_all(piece, "chan", 0, 0, tiled=True)
        owned.append(piece.reshape(chan_size, part, 2, rows, size))
    row_index = lax.broadcasted_iota(jnp.int32, (rows, size), 0) + member * rows
    column_index = lax.broadcasted_iota(jnp.int32, (rows, size), 1)
    packed = jnp.where(column_index >= row_index, spectrum[:, 0], spectrum[:, 1])
    packed, owned[-1] = lax.optimization_barrier((packed, owned[-1]))
    if chunks > 1:
        packed = packed.reshape(chunks, chan_size, part, rows, size).transpose(1, 0, 2, 3, 4)
    packed = packed.reshape(group_bins, rows, size)
    packed = lax.all_to_all(packed, "chan", 0, 0, tiled=True)
    packed = packed.reshape(chan_size, own, rows, size)
    table = projection_table(lag_cutoff[0], count, freq_size, chan_size, chunks)

    middles = []
    for chunk in range(chunks):
        scale = lax.dynamic_slice_in_dim(
            guess_scale, chunk * part * chan_size + member * part, part, 0
        )
        inverse = pl.pallas_call(
            newton_kernel,
            grid=(part // step,),
            in_specs=[pl.BlockSpec(memory_space=pltpu.SMEM), panel_block],
            out_specs=inverse_block,
            out_shape=jax.ShapeDtypeStruct((part, 2, size, 2 * size), BF16),
            compiler_params=params(16),
            cost_estimate=cost(part * 64 * 2 * 4 * size**3, part * 6 * 4 * size * size),
        )(scale, owned[chunk])
        offset = chunk * (part // step)
        middles.append(
            pl.pallas_call(
                middle_kernel,
                grid=(part // step,),
                in_specs=[
                    inverse_block,
                    pl.BlockSpec(
                        (chan_size, step, rows, size), lambda i, offset=offset: (0, i + offset, 0, 0)
                    ),
                ],
                out_specs=pl.BlockSpec((size * part, size), lambda i: (0, 0)),
                out_shape=jax.ShapeDtypeStruct((size * part, size), F32),
                compiler_params=params(16),
                cost_estimate=cost(part * 10 * 2 * 4 * size**3, part * 6 * 4 * size * size),
            )(inverse, packed)
        )

    middles = [middle.astype(jnp.float16).reshape(size, part, size) for middle in middles]
    sent = cat(middles, 1) if chunks > 1 else middles[0]
    if lane_parts > 1:
        sent = sent.reshape(size, own, lane_parts, lanes).transpose(0, 2, 1, 3)
    sent = sent.reshape(devices, kept, own, lanes)
    values = lax.all_to_all(sent, ("chan", "freq"), 0, 0, tiled=True).astype(F32)
    sources, own_rows = devices, own
    if own % 8:
        values = values.transpose(1, 0, 2, 3).reshape(1, kept, count, lanes)
        sources, own_rows = 1, count
    pair = math.gcd(kept, 2)
    causal = pl.pallas_call(
        causal_kernel,
        grid=(kept // pair,),
        in_specs=[
            pl.BlockSpec((2, count, count), lambda i: (0, 0, 0)),
            pl.BlockSpec((sources, pair, own_rows, lanes), lambda i: (0, i, 0, 0)),
        ],
        out_specs=pl.BlockSpec((sources, pair, 2, own_rows, lanes), lambda i: (0, i, 0, 0, 0)),
        out_shape=jax.ShapeDtypeStruct((sources, kept, 2, own_rows, lanes), F32),
        scratch_shapes=[pltpu.VMEM((2 * count, count), BF16), pltpu.VMEM((2 * count, count), BF16)],
        compiler_params=params(24),
        cost_estimate=cost(kept * 12 * count * count * lanes, 12 * kept * count * lanes),
    )(table, values)
    causal = causal.astype(jnp.float16)
    if own % 8:
        causal = causal.reshape(kept, 2, devices, own, lanes).transpose(2, 0, 1, 3, 4)

    pieces = []
    for chunk in range(chunks):
        back = causal[:, :, :, chunk * part : (chunk + 1) * part]
        back = lax.all_to_all(back, ("chan", "freq"), 0, 0, tiled=True).astype(F32)
        if lane_parts > 1:
            back = back.reshape(chan_size * column_parts, lane_parts, kept, 2, part, lanes)
            back = back.transpose(0, 2, 3, 4, 1, 5)
        back = back.reshape(size * 2 * part, size)
        result = pl.pallas_call(
            product_kernel,
            grid=(part // step,),
            in_specs=[pl.BlockSpec((size * 2 * part, size), lambda i: (0, 0)), panel_block],
            out_specs=panel_block,
            out_shape=jax.ShapeDtypeStruct((chan_size, part, 2, rows, size), F32),
            compiler_params=params(16),
            cost_estimate=cost(part * 4 * 4 * size**3, part * 5 * 4 * size * size),
        )(back, owned[chunk])
        result = lax.all_to_all(result.astype(jnp.float16), "chan", 0, 0, tiled=True)
        pieces.append(result.reshape(chan_size * part, 2, rows, size))
    whole = cat(pieces, 0) if chunks > 1 else pieces[0]
    return jnp.swapaxes(whole.astype(F32) * SCALE, 2, 3)


def solution(mesh):
    in_specs = (P("freq", None, "chan", None), P("freq", None, "chan", None), P("freq"), P())
    out_specs = P("freq", None, None, "chan")
    body = functools.partial(shards, mesh.shape["freq"], mesh.shape["chan"])
    return jax.shard_map(body, mesh=mesh, in_specs=in_specs, out_specs=out_specs, check_vma=False)
```

profile of v0, /device:TPU:0, one launch (start us, length us, event | category | flops | bytes accessed | tf_op | source)
XLA Modules:
  0.0 145.4 jit_solution(15553517492119560998)
XLA Ops:
  0.0 0.0 copy-start.3
  0.0 0.0 copy-start.2
  0.0 6.4 %all-to-all-start = ((bf16[64,2,32,128]{3,2,1,0:T(8,128)(2,1)}), bf16[64,2,32,128]{3,2,1,0:T(8,128)(2,1)S(1)}, u32[]{:S(2)}, u32[]{:S(2)}) async-start(bf16[64,2,32,128]{3,2,1,0:T(8,128)(2,1)} %param.4), calls=%async_computation | async-start | bytes 2097152 | tf_op jit(solution)/shard_map/all_to_all | solution.py:210
  6.5 0.0 copy-done.3
  6.5 0.1 dynamic_slice.3.scale_ref
  6.5 0.1 iota_compare_fusion
  6.6 0.0 copy-done.2
  6.6 0.8 bitcast_select_fusion
  7.5 24.7 %all-to-all-done = bf16[64,2,32,128]{3,2,1,0:T(8,128)(2,1)S(1)} async-done(((bf16[64,2,32,128]{3,2,1,0:T(8,128)(2,1)}), bf16[64,2,32,128]{3,2,1,0:T(8,128)(2,1)S(1)}, u32[]{:S(2)}, u32[]{:S(2)}) %all-to-all-start) | async-done | bytes 1048608 | tf_op jit(solution)/shard_map/all_to_all | solution.py:210
  32.2 3.5 %all-to-all-start.1 = ((bf16[64,32,128]{2,1,0:T(8,128)(2,1)}), bf16[64,32,128]{2,1,0:T(8,128)(2,1)S(1)}, u32[]{:S(2)}, u32[]{:S(2)}) async-start(bf16[64,32,128]{2,1,0:T(8,128)(2,1)} %bitcast_select_fusion), calls=%async_computation.1 | async-start | bytes 1048576 | tf_op jit(solution)/shard_map/all_to_all | solution.py:219
  35.7 13.0 %shard_map.46.inverse_ref = bf16[16,2,128,256]{3,2,1,0:T(8,128)(2,1)S(1)} custom-call(f32[16]{0:T(128)S(1)} %dynamic_slice.3.scale_ref, bf16[4,16,2,32,128]{4,3,2,1,0:T(8,128)(2,1)S(1)} %bitcast.17), custom_call_target="tpu_custom_call" | custom-call | flops 17179869184 | bytes 6291456 | tf_op jit(solution)/shard_map/pallas_call | solution.py:228
  48.7 0.0 copy-start
  48.7 1.3 copy-done
  50.0 0.0 all-to-all-done.1
  50.0 0.0 copy-start.1
  50.0 1.6 %copy-done.1 = bf16[16,2,128,256]{3,2,1,0:T(8,128)(2,1)S(1)} copy-done((bf16[16,2,128,256]{3,2,1,0:T(8,128)(2,1)S(1)}, bf16[16,2,128,256]{3,2,1,0:T(8,128)(2,1)}, u32[]{:S(2)}) %copy-start.1) | copy-done | bytes 2097176
  51.6 4.9 %shard_map.47 = f32[2048,128]{1,0:T(8,128)S(1)} custom-call(bf16[16,2,128,256]{3,2,1,0:T(8,128)(2,1)S(1)} %copy-done.1, bf16[4,16,32,128]{3,2,1,0:T(8,128)(2,1)S(1)} %bitcast.19), custom_call_target="tpu_custom_call" | custom-call | flops 2684354560 | bytes 6291456 | tf_op jit(solution)/shard_map/pallas_call | solution.py:239
  56.5 0.9 convert_element_type.56
  57.3 6.4 %all-to-all-start.2 = ((f16[32,4,16,128]{3,2,1,0:T(8,128)(2,1)}), f16[32,4,16,128]{3,2,1,0:T(8,128)(2,1)}, u32[]{:S(2)}, u32[]{:S(2)}) async-start(f16[32,4,16,128]{3,2,1,0:T(8,128)(2,1)} %bitcast.6), calls=%async_computation.2 | async-start | bytes 1048576 | tf_op jit(solution)/shard_map/all_to_all | solution.py:260
  64.4 8.2 %fusion.4 = (f32[1,512,512]{2,1,0:T(8,128)S(1)}, f32[1,512,512]{2,1,0:T(8,128)S(1)}) fusion(f32[]{:T(128)} %bitcast, s32[512]{0:T(512)S(1)} %fusion.24, s32[]{:T(128)} %bitcast.1), kind=kLoop, calls=%fused_computation.12 | loop fusion | flops 7340032 | bytes 2099208 | tf_op jit(solution)/shard_map/jit(_where)/select_n | solution.py:175
  72.6 0.2 pad_maximum_fusion.table_ref
  72.8 6.2 %all-to-all-done.2 = f16[32,4,16,128]{3,2,1,0:T(8,128)(2,1)} async-done(((f16[32,4,16,128]{3,2,1,0:T(8,128)(2,1)}), f16[32,4,16,128]{3,2,1,0:T(8,128)(2,1)}, u32[]{:S(2)}, u32[]{:S(2)}) %all-to-all-start.2) | async-done | bytes 524320 | tf_op jit(solution)/shard_map/all_to_all | solution.py:260
  79.1 1.1 convert_element_type.57.values_ref
  80.2 2.5 %shard_map.48 = f32[32,4,2,16,128]{4,3,2,1,0:T(8,128)S(1)} custom-call(f32[2,512,512]{2,1,0:T(8,128)S(1)} %pad_maximum_fusion.table_ref, f32[32,4,16,128]{3,2,1,0:T(8,128)S(1)} %convert_element_type.57.values_ref), custom_call_target="tpu_custom_call" | custom-call | flops 1610612736 | bytes 3145728 | tf_op jit(solution)/shard_map/pallas_call | solution.py:266
  82.7 0.3 convert_element_type.58
  83.0 29.1 %all_to_all.25 = f16[32,4,2,16,128]{4,3,2,1,0:T(8,128)(2,1)S(1)} all-to-all(f16[32,4,2,16,128]{4,3,2,1,0:T(8,128)(2,1)S(1)} %convert_element_type.58), channel_id=1, replica_groups=mesh['freq'=8,'chan'=4] {'chan','freq'}, dimensions={0} | all-to-all | bytes 2097152 | tf_op jit(solution)/shard_map/all_to_all | solution.py:286
  112.1 0.2 bitcast_convert_fusion.causal_ref
  112.3 2.7 %shard_map.49 = f32[4,16,2,32,128]{4,3,2,1,0:T(8,128)S(1)} custom-call(f32[4096,128]{1,0:T(8,128)S(1)} %bitcast_convert_fusion.causal_ref, bf16[4,16,2,32,128]{4,3,2,1,0:T(8,128)(2,1)S(1)} %bitcast.18), custom_call_target="tpu_custom_call" | custom-call | flops 536870912 | bytes 5242880 | tf_op jit(solution)/shard_map/pallas_call | solution.py:291
  115.0 0.3 convert_element_type.59
  115.3 28.5 %all_to_all.26 = f16[4,16,2,32,128]{4,3,2,1,0:T(8,128)(2,1)S(1)} all-to-all(f16[4,16,2,32,128]{4,3,2,1,0:T(8,128)(2,1)S(1)} %convert_element_type.59), channel_id=1, replica_groups=mesh['freq'=8,'chan'=4] {'chan'}, dimensions={0} | all-to-all | bytes 2097152 | tf_op jit(solution)/shard_map/all_to_all | solution.py:300
  143.7 1.6 %convert_multiply_fusion = f32[4,16,2,32,128]{4,3,2,1,0:T(8,128)} fusion(f16[4,16,2,32,128]{4,3,2,1,0:T(8,128)(2,1)S(1)} %all_to_all.26), kind=kLoop, calls=%fused_computation.2 | loop fusion | flops 1048576 | bytes 3145728 | tf_op jit(solution)/shard_map/mul | solution.py:303
  (2 shorter events, 0.0 us)
Async XLA Ops:
  0.0 6.5 %copy-start.3 = (f32[64]{0:T(128)S(1)}, f32[64]{0:T(128)}, u32[]{:S(2)}) copy-start(f32[64]{0:T(128)} %param.6) | copy-start | bytes 772
  0.0 6.6 %copy-start.2 = (bf16[64,2,32,128]{3,2,1,0:T(8,128)(2,1)S(1)}, bf16[64,2,32,128]{3,2,1,0:T(8,128)(2,1)}, u32[]{:S(2)}) copy-start(bf16[64,2,32,128]{3,2,1,0:T(8,128)(2,1)} %param.5) | copy-start | bytes 3145732
  0.0 32.2 %all-to-all-start = ((bf16[64,2,32,128]{3,2,1,0:T(8,128)(2,1)}), bf16[64,2,32,128]{3,2,1,0:T(8,128)(2,1)S(1)}, u32[]{:S(2)}, u32[]{:S(2)}) async-start(bf16[64,2,32,128]{3,2,1,0:T(8,128)(2,1)} %param.4), calls=%async_computation | async-start | bytes 2097152 | tf_op jit(solution)/shard_map/all_to_all | solution.py:210
  32.2 17.8 %all-to-all-start.1 = ((bf16[64,32,128]{2,1,0:T(8,128)(2,1)}), bf16[64,32,128]{2,1,0:T(8,128)(2,1)S(1)}, u32[]{:S(2)}, u32[]{:S(2)}) async-start(bf16[64,32,128]{2,1,0:T(8,128)(2,1)} %bitcast_select_fusion), calls=%async_computation.1 | async-start | bytes 1048576 | tf_op jit(solution)/shard_map/all_to_all | solution.py:219
  48.7 1.3 copy-start
  50.0 1.6 %copy-start.1 = (bf16[16,2,128,256]{3,2,1,0:T(8,128)(2,1)S(1)}, bf16[16,2,128,256]{3,2,1,0:T(8,128)(2,1)}, u32[]{:S(2)}) copy-start(bf16[16,2,128,256]{3,2,1,0:T(8,128)(2,1)} %copy-done) | copy-start | bytes 6291460
  57.3 21.7 %all-to-all-start.2 = ((f16[32,4,16,128]{3,2,1,0:T(8,128)(2,1)}), f16[32,4,16,128]{3,2,1,0:T(8,128)(2,1)}, u32[]{:S(2)}, u32[]{:S(2)}) async-start(f16[32,4,16,128]{3,2,1,0:T(8,128)(2,1)} %bitcast.6), calls=%async_computation.2 | async-start | bytes 1048576 | tf_op jit(solution)/shard_map/all_to_all | solution.py:260
where the time goes:
time: 146 us; the launch traced here: 145 us
  blocking collectives  57.6 us (39%)
  waiting for transfers between devices  31 us (21%)
  Pallas kernels  23.1 us (16%)
  starting transfers between devices  16.3 us (11%)
  other arithmetic  13.7 us (9%)
  local copies, waits for them, and re-layouts  2.99 us (2%)
    all_to_all x1, blocking collectives, shards(): back = lax.all_to_all(back, ('chan', 'freq'), 0, 0, tiled=True).astype(F32)  29.1 us
    all_to_all x1, blocking collectives, shards(): lax.all_to_all(result.astype(jnp.float16), 'chan', 0, 0, tiled=True)  28.5 us
    all_to_all x1, waiting for transfers between devices, shards(): piece = lax.all_to_all(piece, 'chan', 0, 0, tiled=True)  24.7 us
    pallas_call x1, Pallas kernels, shards(): pl.pallas_call(newton_kernel, grid=(part // step,), in_specs=[pl.BlockSpe...  13 us
    select_n x1, other arithmetic, projection_table(): jnp.where(shift == 0, (lag_limit.astype(F32) + 0.5) / count, jnp.sin(last...  8.25 us
    all_to_all x1, starting transfers between devices, shards(): piece = lax.all_to_all(piece, 'chan', 0, 0, tiled=True)  6.45 us
    all_to_all x1, starting transfers between devices, shards(): lax.all_to_all(sent, ('chan', 'freq'), 0, 0, tiled=True).astype(F32)  6.36 us
    all_to_all x1, waiting for transfers between devices, shards(): lax.all_to_all(sent, ('chan', 'freq'), 0, 0, tiled=True).astype(F32)  6.24 us
  transfers between devices with their start and end apart: 3, of which 2 were waited for; matrix products, arithmetic and copies ran while one was open for 6% of the time, Pallas kernels for 9%

commit v1 on v0

--- a/solution.py
+++ b/solution.py
@@ -10,7 +10,7 @@
 
 ITERS = 8
 SCALE = 16.0
-CHUNKS = 1
+CHUNKS = 2
 F32 = jnp.float32
 BF16 = jnp.bfloat16
 MIB = 1024 * 1024

time: 146 us -> 164 us (1.12)
  waiting for transfers between devices: 31 us -> 60.7 us
  blocking collectives: 57.6 us -> 34.8 us
  starting transfers between devices: 16.3 us -> 23.8 us
  local copies, waits for them, and re-layouts: 2.99 us -> 6.54 us
    all_to_all x0 -> x2, waiting for transfers between devices: none -> 26.9 us  [the longest x1 13.5 us: shards(): lax.all_to_all(result.astype(jnp.float16), 'chan', 0, 0, tiled=True)]
    all_to_all x1, blocking collectives: 28.5 us -> 16.4 us  [shards(): lax.all_to_all(result.astype(jnp.float16), 'chan', 0, 0, tiled=True)]
    all_to_all x1, blocking collectives: 29.1 us -> 18.4 us  [shards(): back = lax.all_to_all(back, ('chan', 'freq'), 0, 0, tiled=True).astype(F32)]
    all_to_all x0 -> x2, starting transfers between devices: none -> 6.54 us  [the longest x1 3.47 us: shards(): lax.all_to_all(result.astype(jnp.float16), 'chan', 0, 0, tiled=True)]
    all_to_all x1, waiting for transfers between devices: 0.01 us -> 6.18 us  [shards(): packed = lax.all_to_all(packed, 'chan', 0, 0, tiled=True)]
    slice x0 -> x2, local copies, waits for them, and re-layouts: none -> 3.42 us  [the longest x1 2.33 us: shards(): piece = factor[chunk * part * chan_size:(chunk + 1) * part * chan_size]]
    all_to_all x1 -> x2, starting transfers between devices: 6.45 us -> 9.79 us  [shards(): piece = lax.all_to_all(piece, 'chan', 0, 0, tiled=True)]
    all_to_all x1 -> x2, waiting for transfers between devices: 24.7 us -> 21.4 us  [shards(): piece = lax.all_to_all(piece, 'chan', 0, 0, tiled=True)]
  transfers between devices with their start and end apart: 3 -> 6, of which waited for: 2 -> 6; matrix products, arithmetic and copies ran while one was open for 6% -> 6% of each run, Pallas kernels for 9% -> 10%
where the time goes in v1:
time: 164 us
  waiting for transfers between devices  60.7 us (37%)
  blocking collectives  34.8 us (21%)
  starting transfers between devices  23.8 us (15%)
  Pallas kernels  23.1 us (14%)
  other arithmetic  13.9 us (8%)
  local copies, waits for them, and re-layouts  6.54 us (4%)
    all_to_all x2, waiting for transfers between devices, shards(): piece = lax.all_to_all(piece, 'chan', 0, 0, tiled=True)  21.4 us
    all_to_all x1, blocking collectives, shards(): back = lax.all_to_all(back, ('chan', 'freq'), 0, 0, tiled=True).astype(F32)  18.4 us
    all_to_all x1, blocking collectives, shards(): lax.all_to_all(result.astype(jnp.float16), 'chan', 0, 0, tiled=True)  16.4 us
    pallas_call x2, Pallas kernels, shards(): pl.pallas_call(newton_kernel, grid=(part // step,), in_specs=[pl.BlockSpe...  13.6 us
    all_to_all x1, waiting for transfers between devices, shards(): lax.all_to_all(result.astype(jnp.float16), 'chan', 0, 0, tiled=True)  13.5 us
    all_to_all x1, waiting for transfers between devices, shards(): back = lax.all_to_all(back, ('chan', 'freq'), 0, 0, tiled=True).astype(F32)  13.4 us
    all_to_all x2, starting transfers between devices, shards(): piece = lax.all_to_all(piece, 'chan', 0, 0, tiled=True)  9.79 us
    select_n x1, other arithmetic, projection_table(): jnp.where(shift == 0, (lag_limit.astype(F32) + 0.5) / count, jnp.sin(last...  8.25 us
  transfers between devices with their start and end apart: 6, of which 6 were waited for; matrix products, arithmetic and copies ran while one was open for 6% of the time, Pallas kernels for 10%

profile of v1, /device:TPU:0, one launch (start us, length us, event | category | flops | bytes accessed | tf_op | source)
XLA Modules:
  0.0 163.8 jit_solution(1117180741951303273)
XLA Ops:
  0.0 0.0 copy-start.3
  0.0 0.0 copy-start.2
  0.0 2.3 %fusion.34 = (bf16[32,2,32,128]{3,2,1,0:T(8,128)(2,1)}, bf16[32,2,32,128]{3,2,1,0:T(8,128)(2,1)}) fusion(bf16[64,2,32,128]{3,2,1,0:T(8,128)(2,1)} %param.4), kind=kLoop, calls=%fused_computation.64 | loop fusion | bytes 2097152 | tf_op jit(solution)/shard_map/slice | solution.py:207
  2.3 6.3 %all-to-all-start = ((bf16[32,2,32,128]{3,2,1,0:T(8,128)(2,1)}), bf16[32,2,32,128]{3,2,1,0:T(8,128)(2,1)S(1)}, u32[]{:S(2)}, u32[]{:S(2)}) async-start(bf16[32,2,32,128]{3,2,1,0:T(8,128)(2,1)} %get-tuple-element.15), calls=%async_computation | async-start | bytes 1048576 | tf_op jit(solution)/shard_map/all_to_all | solution.py:210
  8.7 0.0 copy-done.3
  8.7 0.1 fusion.35
  8.7 0.1 iota_compare_fusion
  8.8 0.0 copy-done.2
  8.8 0.1 bitcast_select_fusion
  8.9 14.3 %all-to-all-done = bf16[32,2,32,128]{3,2,1,0:T(8,128)(2,1)S(1)} async-done(((bf16[32,2,32,128]{3,2,1,0:T(8,128)(2,1)}), bf16[32,2,32,128]{3,2,1,0:T(8,128)(2,1)S(1)}, u32[]{:S(2)}, u32[]{:S(2)}) %all-to-all-start) | async-done | bytes 524320 | tf_op jit(solution)/shard_map/all_to_all | solution.py:210
  23.1 3.5 %all-to-all-start.1 = ((bf16[32,2,32,128]{3,2,1,0:T(8,128)(2,1)}), bf16[32,2,32,128]{3,2,1,0:T(8,128)(2,1)S(1)}, u32[]{:S(2)}, u32[]{:S(2)}) async-start(bf16[32,2,32,128]{3,2,1,0:T(8,128)(2,1)} %get-tuple-element.10), calls=%async_computation.1 | async-start | bytes 1048576 | tf_op jit(solution)/shard_map/all_to_all | solution.py:210
  26.6 6.8 %shard_map.46.inverse_ref = bf16[8,2,128,256]{3,2,1,0:T(8,128)(2,1)S(1)} custom-call(f32[8]{0:T(128)S(1)} %get-tuple-element.19.scale_ref, bf16[4,8,2,32,128]{4,3,2,1,0:T(8,128)(2,1)S(1)} %bitcast.27), custom_call_target="tpu_custom_call" | custom-call | flops 8589934592 | bytes 3145728 | tf_op jit(solution)/shard_map/pallas_call | solution.py:228
  33.4 7.2 %all-to-all-done.1 = bf16[32,2,32,128]{3,2,1,0:T(8,128)(2,1)S(1)} async-done(((bf16[32,2,32,128]{3,2,1,0:T(8,128)(2,1)}), bf16[32,2,32,128]{3,2,1,0:T(8,128)(2,1)S(1)}, u32[]{:S(2)}, u32[]{:S(2)}) %all-to-all-start.1) | async-done | bytes 524320 | tf_op jit(solution)/shard_map/all_to_all | solution.py:210
  40.6 0.8 copy.6
  41.4 3.5 %all-to-all-start.2 = ((bf16[64,32,128]{2,1,0:T(8,128)(2,1)}), bf16[64,32,128]{2,1,0:T(8,128)(2,1)S(1)}, u32[]{:S(2)}, u32[]{:S(2)}) async-start(bf16[64,32,128]{2,1,0:T(8,128)(2,1)} %bitcast.8), calls=%async_computation.2 | async-start | bytes 1048576 | tf_op jit(solution)/shard_map/all_to_all | solution.py:219
  44.9 6.8 %shard_map.48.inverse_ref = bf16[8,2,128,256]{3,2,1,0:T(8,128)(2,1)S(1)} custom-call(f32[8]{0:T(128)S(1)} %get-tuple-element.20.scale_ref, bf16[4,8,2,32,128]{4,3,2,1,0:T(8,128)(2,1)S(1)} %bitcast.29), custom_call_target="tpu_custom_call" | custom-call | flops 8589934592 | bytes 3145728 | tf_op jit(solution)/shard_map/pallas_call | solution.py:228
  51.7 0.0 copy-start
  51.7 1.0 copy-done
  52.7 6.2 %all-to-all-done.2 = bf16[64,32,128]{2,1,0:T(8,128)(2,1)S(1)} async-done(((bf16[64,32,128]{2,1,0:T(8,128)(2,1)}), bf16[64,32,128]{2,1,0:T(8,128)(2,1)S(1)}, u32[]{:S(2)}, u32[]{:S(2)}) %all-to-all-start.2) | async-done | bytes 524320 | tf_op jit(solution)/shard_map/all_to_all | solution.py:219
  58.8 0.0 copy-start.1
  58.8 1.2 copy-done.1
  60.1 2.4 %shard_map.49 = f32[1024,128]{1,0:T(8,128)S(1)} custom-call(bf16[8,2,128,256]{3,2,1,0:T(8,128)(2,1)S(1)} %copy-done.1, bf16[4,16,32,128]{3,2,1,0:T(8,128)(2,1)S(1)} %bitcast.31), custom_call_target="tpu_custom_call" | custom-call | flops 1342177280 | bytes 3145728 | tf_op jit(solution)/shard_map/pallas_call | solution.py:239
  62.6 2.5 %shard_map.47 = f32[1024,128]{1,0:T(8,128)S(1)} custom-call(bf16[8,2,128,256]{3,2,1,0:T(8,128)(2,1)S(1)} %shard_map.46.inverse_ref, bf16[4,16,32,128]{3,2,1,0:T(8,128)(2,1)S(1)} %bitcast.32), custom_call_target="tpu_custom_call" | custom-call | flops 1342177280 | bytes 3145728 | tf_op jit(solution)/shard_map/pallas_call | solution.py:239
  65.1 1.0 pad_maximum_fusion.1
  66.1 4.0 %all-to-all-start.3 = ((f16[32,4,16,128]{3,2,1,0:T(8,128)(2,1)}), f16[32,4,16,128]{3,2,1,0:T(8,128)(2,1)}, u32[]{:S(2)}, u32[]{:S(2)}) async-start(f16[32,4,16,128]{3,2,1,0:T(8,128)(2,1)} %pad_maximum_fusion.1), calls=%async_computation.3 | async-start | bytes 1048576 | tf_op jit(solution)/shard_map/all_to_all | solution.py:260
  70.7 8.2 %fusion.4 = (f32[1,512,512]{2,1,0:T(8,128)S(1)}, f32[1,512,512]{2,1,0:T(8,128)S(1)}) fusion(f32[]{:T(128)} %bitcast, s32[512]{0:T(512)S(1)} %fusion.24, s32[]{:T(128)} %bitcast.1), kind=kLoop, calls=%fused_computation.12 | loop fusion | flops 7340032 | bytes 2099208 | tf_op jit(solution)/shard_map/jit(_where)/select_n | solution.py:175
  79.0 0.2 pad_maximum_fusion.table_ref
  79.2 6.2 %all-to-all-done.3 = f16[32,4,16,128]{3,2,1,0:T(8,128)(2,1)} async-done(((f16[32,4,16,128]{3,2,1,0:T(8,128)(2,1)}), f16[32,4,16,128]{3,2,1,0:T(8,128)(2,1)}, u32[]{:S(2)}, u32[]{:S(2)}) %all-to-all-start.3) | async-done | bytes 524320 | tf_op jit(solution)/shard_map/all_to_all | solution.py:260
  85.4 1.1 convert_element_type.64.values_ref
  86.5 2.5 %shard_map.50 = f32[32,4,2,16,128]{4,3,2,1,0:T(8,128)S(1)} custom-call(f32[2,512,512]{2,1,0:T(8,128)S(1)} %pad_maximum_fusion.table_ref, f32[32,4,16,128]{3,2,1,0:T(8,128)S(1)} %convert_element_type.64.values_ref), custom_call_target="tpu_custom_call" | custom-call | flops 1610612736 | bytes 3145728 | tf_op jit(solution)/shard_map/pallas_call | solution.py:266
  89.0 0.3 convert_element_type.65
  89.3 1.1 fusion.33
  90.4 18.4 %all_to_all.40 = f16[32,4,2,8,128]{4,3,2,1,0:T(8,128)(2,1)S(1)} all-to-all(f16[32,4,2,8,128]{4,3,2,1,0:T(8,128)(2,1)S(1)} %get-tuple-element.14), channel_id=1, replica_groups=mesh['freq'=8,'chan'=4] {'chan','freq'}, dimensions={0} | all-to-all | bytes 1048576 | tf_op jit(solution)/shard_map/all_to_all | solution.py:286
  108.8 3.1 %all-to-all-start.4 = ((f16[32,4,2,8,128]{4,3,2,1,0:T(8,128)(2,1)}), f16[32,4,2,8,128]{4,3,2,1,0:T(8,128)(2,1)S(1)}, u32[]{:S(2)}, u32[]{:S(2)}) async-start(f16[32,4,2,8,128]{4,3,2,1,0:T(8,128)(2,1)} %get-tuple-element.13), calls=%async_computation.4 | async-start | bytes 1048576 | tf_op jit(solution)/shard_map/all_to_all | solution.py:286
  111.9 0.1 bitcast_convert_fusion.causal_ref
  112.0 1.1 shard_map.52
  113.1 0.9 convert_element_type.67
  114.0 13.4 %all-to-all-done.4 = f16[32,4,2,8,128]{4,3,2,1,0:T(8,128)(2,1)S(1)} async-done(((f16[32,4,2,8,128]{4,3,2,1,0:T(8,128)(2,1)}), f16[32,4,2,8,128]{4,3,2,1,0:T(8,128)(2,1)S(1)}, u32[]{:S(2)}, u32[]{:S(2)}) %all-to-all-start.4) | async-done | bytes 524320 | tf_op jit(solution)/shard_map/all_to_all | solution.py:286
  127.5 3.5 %all-to-all-start.7 = ((f16[4,8,2,32,128]{4,3,2,1,0:T(8,128)(2,1)}), f16[4,8,2,32,128]{4,3,2,1,0:T(8,128)(2,1)S(1)}, u32[]{:S(2)}, u32[]{:S(2)}) async-start(f16[4,8,2,32,128]{4,3,2,1,0:T(8,128)(2,1)} %convert_element_type.67), calls=%async_computation.7 | async-start | bytes 1048576 | tf_op jit(solution)/shard_map/all_to_all | solution.py:300
  130.9 0.1 bitcast_convert_fusion.1.causal_ref
  131.0 1.1 shard_map.51
  132.1 0.1 convert_element_type.66
  132.3 13.5 %all-to-all-done.7 = f16[4,8,2,32,128]{4,3,2,1,0:T(8,128)(2,1)S(1)} async-done(((f16[4,8,2,32,128]{4,3,2,1,0:T(8,128)(2,1)}), f16[4,8,2,32,128]{4,3,2,1,0:T(8,128)(2,1)S(1)}, u32[]{:S(2)}, u32[]{:S(2)}) %all-to-all-start.7) | async-done | bytes 524320 | tf_op jit(solution)/shard_map/all_to_all | solution.py:300
  145.7 16.4 %all_to_all.41 = f16[4,8,2,32,128]{4,3,2,1,0:T(8,128)(2,1)S(1)} all-to-all(f16[4,8,2,32,128]{4,3,2,1,0:T(8,128)(2,1)S(1)} %convert_element_type.66), channel_id=1, replica_groups=mesh['freq'=8,'chan'=4] {'chan'}, dimensions={0} | all-to-all | bytes 1048576 | tf_op jit(solution)/shard_map/all_to_all | solution.py:300
  162.2 1.6 multiply_bitcast_fusion
  (4 shorter events, 0.1 us)
Async XLA Ops:
  0.0 8.7 %copy-start.3 = (f32[64]{0:T(128)S(1)}, f32[64]{0:T(128)}, u32[]{:S(2)}) copy-start(f32[64]{0:T(128)} %param.6) | copy-start | bytes 772
  0.0 8.8 %copy-start.2 = (bf16[64,2,32,128]{3,2,1,0:T(8,128)(2,1)S(1)}, bf16[64,2,32,128]{3,2,1,0:T(8,128)(2,1)}, u32[]{:S(2)}) copy-start(bf16[64,2,32,128]{3,2,1,0:T(8,128)(2,1)} %param.5) | copy-start | bytes 3145732
  2.3 20.8 %all-to-all-start = ((bf16[32,2,32,128]{3,2,1,0:T(8,128)(2,1)}), bf16[32,2,32,128]{3,2,1,0:T(8,128)(2,1)S(1)}, u32[]{:S(2)}, u32[]{:S(2)}) async-start(bf16[32,2,32,128]{3,2,1,0:T(8,128)(2,1)} %get-tuple-element.15), calls=%async_computation | async-start | bytes 1048576 | tf_op jit(solution)/shard_map/all_to_all | solution.py:210
  23.1 17.4 %all-to-all-start.1 = ((bf16[32,2,32,128]{3,2,1,0:T(8,128)(2,1)}), bf16[32,2,32,128]{3,2,1,0:T(8,128)(2,1)S(1)}, u32[]{:S(2)}, u32[]{:S(2)}) async-start(bf16[32,2,32,128]{3,2,1,0:T(8,128)(2,1)} %get-tuple-element.10), calls=%async_computation.1 | async-start | bytes 1048576 | tf_op jit(solution)/shard_map/all_to_all | solution.py:210
  41.4 17.4 %all-to-all-start.2 = ((bf16[64,32,128]{2,1,0:T(8,128)(2,1)}), bf16[64,32,128]{2,1,0:T(8,128)(2,1)S(1)}, u32[]{:S(2)}, u32[]{:S(2)}) async-start(bf16[64,32,128]{2,1,0:T(8,128)(2,1)} %bitcast.8), calls=%async_computation.2 | async-start | bytes 1048576 | tf_op jit(solution)/shard_map/all_to_all | solution.py:219
  51.7 1.0 copy-start
  58.8 1.2 copy-start.1
  66.1 19.4 %all-to-all-start.3 = ((f16[32,4,16,128]{3,2,1,0:T(8,128)(2,1)}), f16[32,4,16,128]{3,2,1,0:T(8,128)(2,1)}, u32[]{:S(2)}, u32[]{:S(2)}) async-start(f16[32,4,16,128]{3,2,1,0:T(8,128)(2,1)} %pad_maximum_fusion.1), calls=%async_computation.3 | async-start | bytes 1048576 | tf_op jit(solution)/shard_map/all_to_all | solution.py:260
  108.8 18.6 %all-to-all-start.4 = ((f16[32,4,2,8,128]{4,3,2,1,0:T(8,128)(2,1)}), f16[32,4,2,8,128]{4,3,2,1,0:T(8,128)(2,1)S(1)}, u32[]{:S(2)}, u32[]{:S(2)}) async-start(f16[32,4,2,8,128]{4,3,2,1,0:T(8,128)(2,1)} %get-tuple-element.13), calls=%async_computation.4 | async-start | bytes 1048576 | tf_op jit(solution)/shard_map/all_to_all | solution.py:286
  127.5 18.3 %all-to-all-start.7 = ((f16[4,8,2,32,128]{4,3,2,1,0:T(8,128)(2,1)}), f16[4,8,2,32,128]{4,3,2,1,0:T(8,128)(2,1)S(1)}, u32[]{:S(2)}, u32[]{:S(2)}) async-start(f16[4,8,2,32,128]{4,3,2,1,0:T(8,128)(2,1)} %convert_element_type.67), calls=%async_computation.7 | async-start | bytes 1048576 | tf_op jit(solution)/shard_map/all_to_all | solution.py:300
